TPU v7x, 128 devices: a whole 4x4x4 slice. The times are simulated.
128 devices in a mesh: owner: 32 (over x, z, core), seq: 4 (over y).
Axes of the slice: x: 4, y: 4, z: 4, core: 2. Of those that a mesh axis runs over, the one named last changes fastest.
Arguments:
- cand_features: bfloat16 [16384, 1024], P(('owner', 'seq')), may hold values from -6 to 6
- owner_route: int32 [16384], P(('owner', 'seq')), may hold values from 0 to 31, as said below
- hist_lengths: int32 [32], P('owner'), may hold values from 4096 to 16384, as said below
- hist_keys: bfloat16 [32, 16384, 1024], P('owner', 'seq'), may hold values from -6 to 6
- hist_values: bfloat16 [32, 16384, 1024], P('owner', 'seq'), may hold values from -40 to 40
- query_weight: bfloat16 [1024, 1024], replicated, may hold values from -0.1875 to 0.1875
- gate_weight: bfloat16 [1024, 1024], replicated, may hold values from -0.1875 to 0.1875
- out_weight: bfloat16 [1024, 1024], replicated, may hold values from -0.1875 to 0.1875
Outputs:
- ranked: bfloat16 [16384, 1024], P(('owner', 'seq'))
Inputs may be any that keep to these rules, and one draw needn't show every extreme that they name: `owner_route`: among the rows of one device, at most 8 name one owner group; one owner group is named by exactly 8 rows of every device. `hist_lengths`: multiples of 128; some user has 16384.
All inputs are finite; a program needn't handle non-finite values.
Results may differ from a plain program's by a relative error of at most 0.013.
Values may be sent and summed in bfloat16 or wider, within the bound.
A program may use at most 128 MiB of HBM per device.

v0:
```python
import jax
import jax.numpy as jnp
from jax import lax
from jax.sharding import PartitionSpec as P

HEADS = 8
EBLOCK = 512


def event_sum(query_rows, cached_keys, cached_values, length, offset):
    row_count, feature_width = query_rows.shape
    head_width = feature_width // HEADS
    scaling = head_width ** (-0.5)
    query_heads = query_rows.reshape(row_count, HEADS, head_width)
    block_total = cached_keys.shape[0] // EBLOCK
    key_blocks = cached_keys.reshape(block_total, EBLOCK, HEADS, head_width)
    value_blocks = cached_values.reshape(block_total, EBLOCK, HEADS, head_width)

    def add_block(block_id, running):
        key_part = key_blocks[block_id]
        value_part = value_blocks[block_id]
        score = (
            jnp.einsum("chd,ehd->hce", query_heads, key_part, preferred_element_type=jnp.float32)
            * scaling
        )
        position = offset + block_id * EBLOCK + jnp.arange(EBLOCK, dtype=jnp.int32)
        weight = jnp.where(position[None, None, :] < length, jax.nn.silu(score), 0.0).astype(
            jnp.bfloat16
        )
        return running + jnp.einsum(
            "hce,ehd->chd", weight, value_part, preferred_element_type=jnp.float32
        )

    def step_block(block_id, running):
        return add_block(block_id, running)

    start_sum = jnp.zeros((row_count, HEADS, head_width), jnp.float32)
    summed = lax.fori_loop(0, block_total, step_block, start_sum)
    return summed.reshape(row_count, feature_width)


def attend_rows(query_rows, cached_keys, cached_values, length, offset):
    return event_sum(query_rows, cached_keys, cached_values, length, offset)


def body(
    cand_features,
    owner_route,
    hist_lengths,
    hist_keys,
    hist_values,
    query_weight,
    gate_weight,
    out_weight,
):
    local_rows, feature_width = cand_features.shape
    owner_count = lax.axis_size("owner")
    capacity = 2 * local_rows // owner_count
    seq_place = lax.axis_index("seq")
    length = hist_lengths[0]
    cached_keys = hist_keys[0]
    cached_values = hist_values[0]
    offset = seq_place * cached_keys.shape[0]
    targets = jnp.arange(owner_count, dtype=jnp.int32)
    picked = (owner_route[:, None] == targets[None, :]).astype(jnp.int32)
    earlier = jnp.cumsum(picked, axis=0) - picked
    position = jnp.sum(earlier * picked, axis=1)
    send_slot = owner_route * capacity + position
    outgoing = (
        jnp.zeros((owner_count * capacity, feature_width), jnp.bfloat16)
        .at[send_slot]
        .set(cand_features)
    )
    arrived = lax.all_to_all(outgoing, "owner", split_axis=0, concat_axis=0, tiled=True)
    query = jnp.dot(arrived, query_weight, preferred_element_type=jnp.float32).astype(jnp.bfloat16)
    terms = attend_rows(
        lax.all_gather(query, "seq", axis=0, tiled=True), cached_keys, cached_values, length, offset
    )
    attended = lax.psum_scatter(
        terms.astype(jnp.bfloat16), "seq", scatter_dimension=0, tiled=True
    ).astype(jnp.float32)
    gate = jax.nn.silu(jnp.dot(arrived, gate_weight, preferred_element_type=jnp.float32))
    centred = attended - jnp.mean(attended, axis=1, keepdims=True)
    normed = centred * lax.rsqrt(jnp.mean(centred * centred, axis=1, keepdims=True) + 1e-05)
    mixed = (normed * gate).astype(jnp.bfloat16)
    finished = (
        arrived.astype(jnp.float32) + jnp.dot(mixed, out_weight, preferred_element_type=jnp.float32)
    ).astype(jnp.bfloat16)
    returned = lax.all_to_all(finished, "owner", split_axis=0, concat_axis=0, tiled=True)
    return jnp.take(returned, send_slot, axis=0)


def solution(mesh):
    placed = (
        P(("owner", "seq"), None),
        P(("owner", "seq")),
        P("owner"),
        P("owner", "seq", None),
        P("owner", "seq", None),
        P(),
        P(),
        P(),
    )
    return jax.shard_map(
        body, mesh=mesh, in_specs=placed, out_specs=P(("owner", "seq"), None), check_vma=False
    )
```

profile of v0, /device:TPU:1, one launch (start us, length us, event | category | flops | bytes accessed | tf_op | source)
XLA Modules:
  0.0 260.9 jit_solution(4240556070064050137)
XLA Ops:
  11.4 20.9 %all_to_all.24 = bf16[32,8,1024]{2,1,0:T(8,128)(2,1)S(1)} all-to-all(bf16[32,8,1024]{2,1,0:T(8,128)(2,1)S(1)} %bitcast.77), channel_id=1, replica_groups=mesh['owner'=32,'seq'=4] {'owner'}, dimensions={0} | all-to-all | bytes 1048576 | tf_op jit(solution)/shard_map/all_to_all | solution.py:74
  34.7 8.8 %copy.22 = bf16[512,8,8,128]{3,2,1,0:T(8,128)(2,1)} copy(bf16[512,8,8,128]{3,1,2,0:T(8,128)(2,1)} %bitcast.75) | data formatting | bytes 16777216
  43.5 8.8 %copy.23 = bf16[512,8,8,128]{3,2,1,0:T(8,128)(2,1)} copy(bf16[512,8,8,128]{3,1,2,0:T(8,128)(2,1)} %bitcast.76) | data formatting | bytes 16777216
  52.3 10.8 %all-gather.2.cloned.1.call-done = bf16[1024,1024]{1,0:T(8,128)(2,1)} async-done(((bf16[256,1024]{1,0:T(8,128)(2,1)}), bf16[1024,1024]{1,0:T(8,128)(2,1)}) %all-gather.2.cloned.1.call-update) | async-done | bytes 2097168 | tf_op jit(solution)/shard_map/all_gather | solution.py:77
  63.0 3.3 %copy_bitcast_fusion.3 = bf16[1024,8,128]{2,0,1:T(8,128)(2,1)} fusion(bf16[1024,1024]{1,0:T(8,128)(2,1)} %all-gather.2.cloned.1.call-done), kind=kLoop, calls=%fused_computation.19 | loop fusion | bytes 4194304
  66.3 121.9 %while.14 = (s32[]{:T(128)}, f32[1024,8,128]{0,2,1:T(8,128)}, bf16[8,512,8,128]{3,2,1,0:T(8,128)(2,1)}, s32[]{:T(128)}, s32[]{:T(128)}, /*index=5*/bf16[8,512,8,...) while((s32[]{:T(128)}, f32[1024,8,128]{0,2,1:T(8,128)}, ...), condition=%wide.region_4.5_spmd.clone, body=%wide.region_3.4_spmd.clone.sunk | while | flops 2178941952 | bytes 18875540 | solution.py:38
  66.3 2.7 %constant_dynamic-slice_fusion.3 = (bf16[1,512,8,128]{3,2,1,0:T(8,128)(2,1)}, bf16[1,512,8,128]{3,2,1,0:T(8,128)(2,1)S(1)}) fusion(bf16[8,512,8,128]{3,2,1,0:T(8,128)(2,1)} %get-tuple-element.258, s32[]{:T(128)} %get-tuple-element.243, bf16[8,512,8,128]{3,2,1,0:T(8,128)(2,1)} %get-tuple-element.255), kind=kLoop, calls=%fused_computation.14.clone.1 | loop fusion | bytes 4194308 | tf_op jit(solution)/shard_map/while/body/eval_jaxpr/dynamic_slice | solution.py:20
  71.1 9.9 %bitcast_add_fusion.2 = f32[1024,8,128]{0,2,1:T(8,128)} fusion(f32[1024,8,128]{0,2,1:T(8,128)} %get-tuple-element.244, pred[]{:T(512)S(6)} %compare.3, bf16[1024,8,128]{2,0,1:T(8,128)(2,1)} %get-tuple-element.259, pred[512]{0:T(512)(128)(4,1)S(1)} %add_compare_fusion.2, bf16[1,512,8,128]{3,2,1,0:T(8,128)(2,1)} %get-tuple-element.231, ...), kind=kOutput, calls=%fused_computation.9.clone.1 | convolution fusion | flops 2178940928 | bytes 12583425 | tf_op jit(solution)/shard_map/while/body/eval_jaxpr/hce,ehd->chd/dot_general | solution.py:30
  81.0 2.7 %constant_dynamic-slice_fusion.3 = (bf16[1,512,8,128]{3,2,1,0:T(8,128)(2,1)}, bf16[1,512,8,128]{3,2,1,0:T(8,128)(2,1)S(1)}) fusion(bf16[8,512,8,128]{3,2,1,0:T(8,128)(2,1)} %get-tuple-element.258, s32[]{:T(128)} %get-tuple-element.243, bf16[8,512,8,128]{3,2,1,0:T(8,128)(2,1)} %get-tuple-element.255), kind=kLoop, calls=%fused_computation.14.clone.1 | loop fusion | bytes 4194308 | tf_op jit(solution)/shard_map/while/body/eval_jaxpr/dynamic_slice | solution.py:20
  85.8 10.5 %bitcast_add_fusion.2 = f32[1024,8,128]{0,2,1:T(8,128)} fusion(f32[1024,8,128]{0,2,1:T(8,128)} %get-tuple-element.244, pred[]{:T(512)S(6)} %compare.3, bf16[1024,8,128]{2,0,1:T(8,128)(2,1)} %get-tuple-element.259, pred[512]{0:T(512)(128)(4,1)S(1)} %add_compare_fusion.2, bf16[1,512,8,128]{3,2,1,0:T(8,128)(2,1)} %get-tuple-element.231, ...), kind=kOutput, calls=%fused_computation.9.clone.1 | convolution fusion | flops 2178940928 | bytes 12583425 | tf_op jit(solution)/shard_map/while/body/eval_jaxpr/hce,ehd->chd/dot_general | solution.py:30
  96.3 2.7 %constant_dynamic-slice_fusion.3 = (bf16[1,512,8,128]{3,2,1,0:T(8,128)(2,1)}, bf16[1,512,8,128]{3,2,1,0:T(8,128)(2,1)S(1)}) fusion(bf16[8,512,8,128]{3,2,1,0:T(8,128)(2,1)} %get-tuple-element.258, s32[]{:T(128)} %get-tuple-element.243, bf16[8,512,8,128]{3,2,1,0:T(8,128)(2,1)} %get-tuple-element.255), kind=kLoop, calls=%fused_computation.14.clone.1 | loop fusion | bytes 4194308 | tf_op jit(solution)/shard_map/while/body/eval_jaxpr/dynamic_slice | solution.py:20
  101.1 10.5 %bitcast_add_fusion.2 = f32[1024,8,128]{0,2,1:T(8,128)} fusion(f32[1024,8,128]{0,2,1:T(8,128)} %get-tuple-element.244, pred[]{:T(512)S(6)} %compare.3, bf16[1024,8,128]{2,0,1:T(8,128)(2,1)} %get-tuple-element.259, pred[512]{0:T(512)(128)(4,1)S(1)} %add_compare_fusion.2, bf16[1,512,8,128]{3,2,1,0:T(8,128)(2,1)} %get-tuple-element.231, ...), kind=kOutput, calls=%fused_computation.9.clone.1 | convolution fusion | flops 2178940928 | bytes 12583425 | tf_op jit(solution)/shard_map/while/body/eval_jaxpr/hce,ehd->chd/dot_general | solution.py:30
  111.6 2.7 %constant_dynamic-slice_fusion.3 = (bf16[1,512,8,128]{3,2,1,0:T(8,128)(2,1)}, bf16[1,512,8,128]{3,2,1,0:T(8,128)(2,1)S(1)}) fusion(bf16[8,512,8,128]{3,2,1,0:T(8,128)(2,1)} %get-tuple-element.258, s32[]{:T(128)} %get-tuple-element.243, bf16[8,512,8,128]{3,2,1,0:T(8,128)(2,1)} %get-tuple-element.255), kind=kLoop, calls=%fused_computation.14.clone.1 | loop fusion | bytes 4194308 | tf_op jit(solution)/shard_map/while/body/eval_jaxpr/dynamic_slice | solution.py:20
  116.4 10.5 %bitcast_add_fusion.2 = f32[1024,8,128]{0,2,1:T(8,128)} fusion(f32[1024,8,128]{0,2,1:T(8,128)} %get-tuple-element.244, pred[]{:T(512)S(6)} %compare.3, bf16[1024,8,128]{2,0,1:T(8,128)(2,1)} %get-tuple-element.259, pred[512]{0:T(512)(128)(4,1)S(1)} %add_compare_fusion.2, bf16[1,512,8,128]{3,2,1,0:T(8,128)(2,1)} %get-tuple-element.231, ...), kind=kOutput, calls=%fused_computation.9.clone.1 | convolution fusion | flops 2178940928 | bytes 12583425 | tf_op jit(solution)/shard_map/while/body/eval_jaxpr/hce,ehd->chd/dot_general | solution.py:30
  131.8 10.5 %bitcast_add_fusion.2 = f32[1024,8,128]{0,2,1:T(8,128)} fusion(f32[1024,8,128]{0,2,1:T(8,128)} %get-tuple-element.244, pred[]{:T(512)S(6)} %compare.3, bf16[1024,8,128]{2,0,1:T(8,128)(2,1)} %get-tuple-element.259, pred[512]{0:T(512)(128)(4,1)S(1)} %add_compare_fusion.2, bf16[1,512,8,128]{3,2,1,0:T(8,128)(2,1)} %get-tuple-element.231, ...), kind=kOutput, calls=%fused_computation.9.clone.1 | convolution fusion | flops 2178940928 | bytes 12583425 | tf_op jit(solution)/shard_map/while/body/eval_jaxpr/hce,ehd->chd/dot_general | solution.py:30
  147.1 10.5 %bitcast_add_fusion.2 = f32[1024,8,128]{0,2,1:T(8,128)} fusion(f32[1024,8,128]{0,2,1:T(8,128)} %get-tuple-element.244, pred[]{:T(512)S(6)} %compare.3, bf16[1024,8,128]{2,0,1:T(8,128)(2,1)} %get-tuple-element.259, pred[512]{0:T(512)(128)(4,1)S(1)} %add_compare_fusion.2, bf16[1,512,8,128]{3,2,1,0:T(8,128)(2,1)} %get-tuple-element.231, ...), kind=kOutput, calls=%fused_computation.9.clone.1 | convolution fusion | flops 2178940928 | bytes 12583425 | tf_op jit(solution)/shard_map/while/body/eval_jaxpr/hce,ehd->chd/dot_general | solution.py:30
  162.4 10.5 %bitcast_add_fusion.2 = f32[1024,8,128]{0,2,1:T(8,128)} fusion(f32[1024,8,128]{0,2,1:T(8,128)} %get-tuple-element.244, pred[]{:T(512)S(6)} %compare.3, bf16[1024,8,128]{2,0,1:T(8,128)(2,1)} %get-tuple-element.259, pred[512]{0:T(512)(128)(4,1)S(1)} %add_compare_fusion.2, bf16[1,512,8,128]{3,2,1,0:T(8,128)(2,1)} %get-tuple-element.231, ...), kind=kOutput, calls=%fused_computation.9.clone.1 | convolution fusion | flops 2178940928 | bytes 12583425 | tf_op jit(solution)/shard_map/while/body/eval_jaxpr/hce,ehd->chd/dot_general | solution.py:30
  177.7 10.5 %bitcast_add_fusion.2 = f32[1024,8,128]{0,2,1:T(8,128)} fusion(f32[1024,8,128]{0,2,1:T(8,128)} %get-tuple-element.244, pred[]{:T(512)S(6)} %compare.3, bf16[1024,8,128]{2,0,1:T(8,128)(2,1)} %get-tuple-element.259, pred[512]{0:T(512)(128)(4,1)S(1)} %add_compare_fusion.2, bf16[1,512,8,128]{3,2,1,0:T(8,128)(2,1)} %get-tuple-element.231, ...), kind=kOutput, calls=%fused_computation.9.clone.1 | convolution fusion | flops 2178940928 | bytes 12583425 | tf_op jit(solution)/shard_map/while/body/eval_jaxpr/hce,ehd->chd/dot_general | solution.py:30
  188.2 3.9 %convert_element_type.34 = bf16[1024,8,128]{0,2,1:T(8,128)(2,1)} convert(f32[1024,8,128]{0,2,1:T(8,128)} %get-tuple-element.129) | non-fusion elementwise | flops 1048576 | bytes 6291456 | tf_op jit(solution)/shard_map/convert_element_type | solution.py:80
  192.1 4.0 %copy.18 = bf16[1024,1024]{1,0:T(8,128)(2,1)} copy(bf16[1024,1024]{0,1:T(8,128)(2,1)} %bitcast.74) | data formatting | bytes 4194304 | tf_op jit(solution)/shard_map/convert_element_type | solution.py:80
  196.1 29.9 %reduce-scatter.2.cloned.1.call-done = bf16[256,1024]{1,0:T(8,128)(2,1)} async-done(((bf16[1024,1024]{1,0:T(8,128)(2,1)}), bf16[256,1024]{1,0:T(8,128)(2,1)}) %reduce-scatter.2.cloned.1.call-update) | async-done | bytes 524304 | tf_op jit(solution)/shard_map/reduce_scatter | solution.py:79
  228.6 4.6 %fusion.13 = bf16[32,8,1024]{2,1,0:T(8,128)(2,1)} fusion(bf16[1024,1024]{1,0:T(8,128)(2,1)} %param.17, bf16[256,1024]{1,0:T(8,128)(2,1)} %reduce-scatter.2.cloned.1.call-done, bf16[32,8,1024]{2,1,0:T(8,128)(2,1)S(1)} %copy-done.2, bf16[1024,1024]{1,0:T(8,128)(2,1)} %param.16, f32[256]{0:T(256)S(1)} %add_rsqrt_fusion, f32[256]{0:T(256)S(1)} %broadcast_multiply_fusion), kind=kOutput, calls=%fused_computation.27 | convolution fusion | flops 1076887552 | bytes 5769216 | tf_op jit(solution)/shard_map/dot_general | solution.py:87
  233.2 7.6 %all-to-all-start.1 = ((bf16[32,8,1024]{2,1,0:T(8,128)(2,1)}), bf16[32,8,1024]{2,1,0:T(8,128)(2,1)S(1)}, u32[]{:S(2)}, u32[]{:S(2)}) async-start(bf16[32,8,1024]{2,1,0:T(8,128)(2,1)} %fusion.13), calls=%async_computation.2 | async-start | bytes 1048576 | tf_op jit(solution)/shard_map/all_to_all | solution.py:89
  240.8 11.6 %all-to-all-done.1 = bf16[32,8,1024]{2,1,0:T(8,128)(2,1)S(1)} async-done(((bf16[32,8,1024]{2,1,0:T(8,128)(2,1)}), bf16[32,8,1024]{2,1,0:T(8,128)(2,1)S(1)}, u32[]{:S(2)}, u32[]{:S(2)}) %all-to-all-start.1) | async-done | bytes 524320 | tf_op jit(solution)/shard_map/all_to_all | solution.py:89
  (50 shorter events, 39.2 us)
Async XLA Ops:
  6.5 26.5 %copy-start = (bf16[1024,1024]{1,0:T(8,128)(2,1)S(1)}, bf16[1024,1024]{1,0:T(8,128)(2,1)}, u32[]{:S(2)}) copy-start(bf16[1024,1024]{1,0:T(8,128)(2,1)} %param.15) | copy-start | bytes 6291460
  6.5 56.5 %all-gather.2.cloned.1.call-start = ((), (), s32[]{:S(2)}) async-start(), calls=%async_computation.3 | async-start | bytes 2621440 | tf_op jit(solution)/shard_map/all_gather | solution.py:77
  9.6 33.9 %copy-start.4 = (s32[128]{0:T(128)}, s32[128]{0:T(128)S(1)}, u32[]{:S(2)}) copy-start(s32[128]{0:T(128)S(1)} %get-tuple-element.183) | copy-start | bytes 1540
  32.2 0.8 copy-start.1
  34.6 191.4 %reduce-scatter.2.cloned.1.call-start = ((), (), s32[]{:S(2)}) async-start(), calls=%async_computation.4 | async-start | bytes 2621440 | tf_op jit(solution)/shard_map/reduce_scatter | solution.py:79
  192.1 36.5 %copy-start.2 = (bf16[32,8,1024]{2,1,0:T(8,128)(2,1)S(1)}, bf16[32,8,1024]{2,1,0:T(8,128)(2,1)}, u32[]{:S(2)}) copy-start(bf16[32,8,1024]{2,1,0:T(8,128)(2,1)} %copy-done.1) | copy-start | bytes 1572868
  228.5 12.3 %copy-start.5 = (s32[128]{0:T(128)S(1)}, s32[128]{0:T(128)}, u32[]{:S(2)}) copy-start(s32[128]{0:T(128)} %copy-done.4) | copy-start | bytes 1540
  228.5 24.7 %copy-start.3 = (pred[128]{0:T(512)(128)(4,1)S(1)}, pred[128]{0:T(512)(128)(4,1)}, u32[]{:S(2)}) copy-start(pred[128]{0:T(512)(128)(4,1)} %get-tuple-element.182) | copy-start | bytes 388
  233.2 19.2 %all-to-all-start.1 = ((bf16[32,8,1024]{2,1,0:T(8,128)(2,1)}), bf16[32,8,1024]{2,1,0:T(8,128)(2,1)S(1)}, u32[]{:S(2)}, u32[]{:S(2)}) async-start(bf16[32,8,1024]{2,1,0:T(8,128)(2,1)} %fusion.13), calls=%async_computation.2 | async-start | bytes 1048576 | tf_op jit(solution)/shard_map/all_to_all | solution.py:89
Sparse Core Ops, SparseCore 0:
  34.7 28.2 all-gather.1
  196.2 29.7 reduce-scatter.1
where the time goes:
time: 262 us; the launch traced here: 261 us
  matrix products  89.5 us (34%)
  local copies, waits for them, and re-layouts  61.6 us (24%)
  waiting for transfers between devices  52.3 us (20%)
  blocking collectives  20.9 us (8%)
  other arithmetic  15.5 us (6%)
  between operations  13.5 us (5%)
  starting transfers between devices  7.66 us (3%)
    dot_general x8, matrix products, add_block(): jnp.einsum('hce,ehd->chd', weight, value_part, preferred_element_type=jnp...  83.4 us
    reduce_scatter x1, waiting for transfers between devices, body(): lax.psum_scatter(terms.astype(jnp.bfloat16), 'seq', scatter_dimension=0,...  29.9 us
    unnamed x15, local copies, waits for them, and re-layouts  21.7 us
    dynamic_slice x8, local copies, waits for them, and re-layouts, add_block(): key_part = key_blocks[block_id]  21.4 us
    all_to_all x1, blocking collectives, body(): lax.all_to_all(outgoing, 'owner', split_axis=0, concat_axis=0, tiled=True)  20.9 us
    dynamic_slice x8, local copies, waits for them, and re-layouts, add_block(): value_part = value_blocks[block_id]  11.8 us
    all_to_all x1, waiting for transfers between devices, body(): lax.all_to_all(finished, 'owner', split_axis=0, concat_axis=0, tiled=True)  11.6 us
    all_gather x1, waiting for transfers between devices, body(): lax.all_gather(query, 'seq', axis=0, tiled=True)  10.8 us
  transfers between devices with their start and end apart: 3, of which 3 were waited for; matrix products, arithmetic and copies ran while one was open for 7% of the time, Pallas kernels for 0%

commit v1 on v0

v1 whole, which is shorter than its diff:
```python
import functools

import jax
import jax.numpy as jnp
from jax import lax
from jax.experimental import pallas as pl
from jax.experimental.pallas import tpu as pltpu
from jax.sharding import PartitionSpec as P

HEADS = 8
CAP = 8
FOLD = 2
PIECE = CAP * FOLD
RING = 4
CHUNKS = 4
EVENT_BLOCK = 1024
MESH = pl.DeviceIdType.MESH
F32 = jnp.float32
BF16 = jnp.bfloat16


def dot(a, b):
    return jnp.dot(a, b, preferred_element_type=F32)


def layer_kernel(
    owners,
    length_ref, cand_ref, route_ref, wq_hbm, wg_hbm, wo_hbm, k_hbm, v_hbm,
    out_ref,
    keys, raw, vt, wq, wg, wo, fold, xc, part, pf, gl, gr, rl, rr, tot, ret, gate,
    load_sem, in_send, in_recv, x_send, x_recv, p_send, gl_recv, gr_recv, rl_recv, rr_recv,
    r_send, r_recv,
):
    me = lax.axis_index("owner")
    seq = lax.axis_index("seq")
    right, left = lax.rem(seq + 1, RING), lax.rem(seq + RING - 1, RING)
    per = owners // 4
    rows, width = cand_ref.shape
    half = width // FOLD
    head = width // HEADS
    events = keys.shape[0]
    block = min(EVENT_BLOCK, events)
    span = per * CAP

    loads = [
        pltpu.make_async_copy(src, dst, load_sem.at[i])
        for i, (src, dst) in enumerate(
            [(wq_hbm, wq), (v_hbm.at[0], raw), (wg_hbm, wg), (k_hbm.at[0], keys), (wo_hbm, wo)]
        )
    ]
    load_wq, load_v, load_wg, load_k, load_wo = loads
    for load in loads:
        load.start()

    barrier = pltpu.get_barrier_semaphore()

    def greet(i, carry):
        other = lax.rem(me + i, owners)
        pl.semaphore_signal(barrier, inc=1, device_id=(other, seq), device_id_type=MESH)
        return carry

    lax.fori_loop(1, owners, greet, 0)
    for other in (left, right):
        pl.semaphore_signal(barrier, inc=1, device_id=(me, other), device_id_type=MESH)

    def remote(src, dst, send, recv, owner, place):
        return pltpu.make_async_remote_copy(
            src_ref=src, dst_ref=dst, send_sem=send, recv_sem=recv,
            device_id=(owner, place), device_id_type=MESH,
        )

    def await_bytes(ref, sem):
        pltpu.make_async_copy(ref, ref, sem).wait()

    route_lane = jnp.broadcast_to(route_ref[...].astype(F32), (rows, rows))
    route_row = jnp.transpose(route_lane)
    lane = lax.broadcasted_iota(jnp.int32, (rows, rows), 1)
    sub = lax.broadcasted_iota(jnp.int32, (rows, rows), 0)
    same = route_lane == route_row
    before = jnp.sum(jnp.where(same & (sub < lane), 1.0, 0.0), axis=0, keepdims=True)
    place_lane = (route_ref[...].astype(F32) * PIECE + before).astype(jnp.int32)
    slot = lax.broadcasted_iota(jnp.int32, (owners * PIECE, rows), 0)

    load_wq.wait()
    scale = 0.5 * head ** (-0.5)
    query = (dot(cand_ref[...], wq[...]) * scale).astype(BF16)
    packed = sum(
        dot(
            jnp.where(slot == place_lane + CAP * f, 1.0, 0.0).astype(BF16),
            query[:, f * half:(f + 1) * half],
        )
        for f in range(FOLD)
    )
    fold[...] = packed.astype(BF16)

    pl.semaphore_wait(barrier, owners + 1)

    quarter = me // per
    spot = pl.ds(pl.multiple_of(lax.rem(me, per) * PIECE, PIECE), PIECE)
    home = xc.at[3 * lax.rem(quarter, 2), quarter // 2, spot, :]

    def piece(ref, owner):
        return ref.at[pl.ds(pl.multiple_of(owner * PIECE, PIECE), PIECE), :]

    def scatter(i, carry):
        other = lax.rem(me + i, owners)
        remote(piece(fold, other), home, in_send.at[0], in_recv.at[quarter], other, seq).start()
        return carry

    lax.fori_loop(1, owners, scatter, 0)
    pltpu.make_async_copy(piece(fold, me), home, in_recv.at[quarter]).start()

    load_wg.wait()
    gated = dot(cand_ref[...], wg[...])
    gate[...] = gated / (1.0 + jnp.exp(-gated))

    load_v.wait()
    limit = length_ref[0] - seq * events

    def turn(i, carry):
        at = pl.ds(pl.multiple_of(i * block, block), block)
        event = i * block + lax.broadcasted_iota(jnp.int32, (block, head), 0)
        for h in range(HEADS):
            cols = slice(h * head, (h + 1) * head)
            values = jnp.where(event < limit, raw[at, cols].astype(F32), 0.0)
            vt[cols, at] = jnp.transpose(values).astype(BF16)
        return carry

    turns = events // block
    lax.fori_loop(0, turns // 2, turn, 0)

    own = {0: (0, 0), 2: (0, 1), 1: (3, 0), 3: (3, 1)}
    to_right = {0: (0, 2), 1: (1, 0), 2: (2, 0), 3: (3, 2)}
    to_left = {2: (0, 3), 3: (1, 1), 0: (2, 1), 1: (3, 3)}

    def pass_on(source, dest, send, place):
        c, j = dest
        remote(
            xc.at[source[0], source[1]], xc.at[c, j], x_send.at[send], x_recv.at[c * 4 + j],
            me, place,
        ).start()

    def await_block(c, j):
        await_bytes(xc.at[c, j], x_recv.at[c * 4 + j])

    for rq, lq in ((0, 2), (1, 3)):
        for q in (rq, lq):
            await_bytes(xc.at[own[q][0], own[q][1]], in_recv.at[q])
        pass_on(own[rq], to_right[rq], rq, right)
        pass_on(own[lq], to_left[lq], 6 + lq, left)

    lax.fori_loop(turns // 2, turns, turn, 0)
    load_k.wait()

    def before_chunk(c):
        if c == 0:
            await_block(0, 2)
            await_block(0, 3)
            pass_on((0, 2), (1, 2), 4, right)
            pass_on((0, 3), (1, 3), 10, left)
            for rq, lq in ((2, 0), (3, 1)):
                pass_on(own[rq], to_right[rq], rq, right)
                pass_on(own[lq], to_left[lq], 6 + lq, left)
        if c == 1:
            for j in range(4):
                await_block(1, j)
            pass_on((1, 0), (2, 2), 5, right)
            pass_on((1, 1), (2, 3), 11, left)
        if c == 2:
            for j in range(4):
                await_block(2, j)
        if c == 3:
            await_block(3, 2)
            await_block(3, 3)

    def give(c, j, dest, recv, send, place):
        remote(part.at[c, j], dest, p_send.at[send], recv, me, place).start()

    def add(c, j, ref, at, sem):
        await_bytes(ref.at[at], sem.at[at])
        part[c, j] = (part[c, j].astype(F32) + ref[at].astype(F32)).astype(BF16)

    def after_chunk(c):
        if c == 0:
            give(0, 3, gl.at[2], gl_recv.at[2], 0, right)
            give(0, 2, gr.at[0], gr_recv.at[0], 6, left)
        if c == 1:
            give(1, 2, rl.at[0], rl_recv.at[0], 1, right)
            give(1, 3, rr.at[0], rr_recv.at[0], 7, left)
            give(1, 1, gl.at[3], gl_recv.at[3], 2, right)
            give(1, 0, gr.at[1], gr_recv.at[1], 8, left)
        if c == 2:
            give(2, 2, rl.at[1], rl_recv.at[1], 3, right)
            give(2, 3, rr.at[1], rr_recv.at[1], 9, left)
            add(2, 1, rl, 0, rl_recv)
            give(2, 1, gl.at[0], gl_recv.at[0], 4, right)
            add(2, 0, rr, 0, rr_recv)
            give(2, 0, gr.at[2], gr_recv.at[2], 10, left)
        if c == 3:
            add(3, 3, rl, 1, rl_recv)
            give(3, 3, gl.at[1], gl_recv.at[1], 5, right)
            add(3, 2, rr, 1, rr_recv)
            give(3, 2, gr.at[3], gr_recv.at[3], 11, left)

    def attend(c):
        def columns(h):
            f, cols = h // (HEADS // FOLD), slice(h % (HEADS // FOLD) * head, (h % (HEADS // FOLD) + 1) * head)
            parts = [
                xc[c, j, :, cols].astype(F32).reshape(per, FOLD, CAP, head)[:, f].reshape(span, head)
                for j in range(4)
            ]
            return jnp.transpose(jnp.concatenate(parts, axis=0)).astype(BF16)

        def weigh(h, e, turned):
            score = dot(keys[e * block:(e + 1) * block, h * head:(h + 1) * head], turned)
            return (score + score * jnp.tanh(score)).astype(BF16)

        def finish(h, total):
            f, cols = h // (HEADS // FOLD), slice(h % (HEADS // FOLD) * head, (h % (HEADS // FOLD) + 1) * head)
            back = jnp.transpose(total)
            for j in range(4):
                pf[j, :, f, :, cols] = back[j * span:(j + 1) * span].reshape(per, CAP, head)

        waiting = None
        totals = {}

        def settle(h, e, weight):
            term = dot(vt[h * head:(h + 1) * head, e * block:(e + 1) * block], weight)
            totals[h] = totals[h] + term if e else term
            if e == events // block - 1:
                finish(h, totals.pop(h))

        for h in range(HEADS):
            turned = columns(h)
            for e in range(events // block):
                weight = weigh(h, e, turned)
                if waiting is not None:
                    settle(*waiting)
                waiting = (h, e, weight)
        settle(*waiting)
        for j in range(4):
            part[c, j] = pf[j].reshape(per * PIECE, half).astype(BF16)

    def step(c, carry):
        for now in range(CHUNKS):
            pl.when(c == now)(functools.partial(before_chunk, now))
        attend(c)
        for now in range(CHUNKS):
            pl.when(c == now)(functools.partial(after_chunk, now))
        return carry

    lax.fori_loop(0, CHUNKS, step, 0)

    landing = piece(ret, me)
    for q in (0, 2, 1, 3):
        await_bytes(gl.at[q], gl_recv.at[q])
        await_bytes(gr.at[q], gr_recv.at[q])
        mine = part[own[q][0], own[q][1]].astype(F32)
        tot[q] = (mine + gl[q].astype(F32) + gr[q].astype(F32)).astype(BF16)

        def hand_back(i, carry, q=q):
            spot = lax.rem(me + i, per)
            other = q * per + spot
            source = tot.at[q, pl.ds(pl.multiple_of(spot * PIECE, PIECE), PIECE), :]

            @pl.when(other == me)
            def _():
                pltpu.make_async_copy(source, landing, r_recv.at[0]).start()

            @pl.when(other != me)
            def _():
                remote(source, landing, r_send.at[0], r_recv.at[0], other, seq).start()

            return carry

        lax.fori_loop(0, per, hand_back, 0)

    place_row = jnp.transpose(
        jnp.broadcast_to(place_lane.astype(F32), (rows, rows))
    ).astype(jnp.int32)[:, :1]
    slot_lane = lax.broadcasted_iota(jnp.int32, (rows, owners * PIECE), 1)
    picks = [
        jnp.where(slot_lane == place_row + CAP * f, 1.0, 0.0).astype(BF16) for f in range(FOLD)
    ]
    load_wo.wait()

    await_bytes(ret, r_recv.at[0])
    attended = jnp.concatenate([dot(pick, ret[...]) for pick in picks], axis=1)
    centred = attended - jnp.mean(attended, axis=1, keepdims=True)
    normed = centred * lax.rsqrt(jnp.mean(centred * centred, axis=1, keepdims=True) + 1e-05)
    mixed = (normed * gate[...]).astype(BF16)
    out_ref[...] = (cand_ref[...].astype(F32) + dot(mixed, wo[...])).astype(BF16)

    sent = (owners - 1) * PIECE
    await_bytes(fold.at[pl.ds(0, sent), :], in_send.at[0])
    await_bytes(ret.at[pl.ds(0, sent), :], r_send.at[0])
    for i in range(12):
        await_bytes(xc.at[0, 0], x_send.at[i])
        await_bytes(part.at[0, 0], p_send.at[i])


def body(cand, route, lengths, keys, values, wq, wg, wo):
    owners = lax.axis_size("owner")
    rows, width = cand.shape
    events = keys.shape[1]
    half = width // FOLD
    per = owners // 4
    square = pltpu.VMEM((width, width), BF16)
    slots = pltpu.VMEM((owners * PIECE, half), BF16)
    blocks = lambda *lead: pltpu.VMEM((*lead, per * PIECE, half), BF16)
    sems = lambda n: pltpu.SemaphoreType.DMA((n,))
    vmem = pl.BlockSpec(memory_space=pltpu.VMEM)
    hbm = pl.BlockSpec(memory_space=pl.ANY)
    return pl.pallas_call(
        functools.partial(layer_kernel, owners),
        out_shape=jax.ShapeDtypeStruct((rows, width), BF16),
        in_specs=[pl.BlockSpec(memory_space=pltpu.SMEM), vmem, vmem, hbm, hbm, hbm, hbm, hbm],
        out_specs=vmem,
        scratch_shapes=[
            pltpu.VMEM((events, width), BF16),
            pltpu.VMEM((events, width), BF16),
            pltpu.VMEM((width, events), BF16),
            square, square, square,
            slots,
            blocks(CHUNKS, 4),
            blocks(CHUNKS, 4),
            pltpu.VMEM((4, per, FOLD, CAP, half), F32),
            blocks(4), blocks(4), blocks(2), blocks(2), blocks(4),
            slots,
            pltpu.VMEM((rows, width), F32),
            sems(5), sems(1), sems(4), sems(12), sems(16), sems(12),
            sems(4), sems(4), sems(2), sems(2), sems(1), sems(1),
        ],
        compiler_params=pltpu.CompilerParams(
            collective_id=0, has_side_effects=True, vmem_limit_bytes=56 * 2**20
        ),
        name="candidate_layer",
    )(lengths, cand, route.reshape(1, rows), wq, wg, wo, keys, values)


def solution(mesh):
    placed = (
        P(("owner", "seq"), None),
        P(("owner", "seq")),
        P("owner"),
        P("owner", "seq", None),
        P("owner", "seq", None),
        P(),
        P(),
        P(),
    )
    return jax.shard_map(
        body, mesh=mesh, in_specs=placed, out_specs=P(("owner", "seq"), None), check_vma=False
    )
```

time: 262 us -> 72 us (0.27)
  the two profiles are of different devices: /device:TPU:1 before, /device:TPU:3 now
where the time goes in v1:
time: 72 us; the launch traced here: 71.9 us
  Pallas kernels  69.5 us (97%)
  local copies, waits for them, and re-layouts  1.67 us (2%)
    pallas_call x1, Pallas kernels, body(): pl.pallas_call(functools.partial(layer_kernel, owners), out_shape=jax.Sha...  69.5 us
    unnamed x1, local copies, waits for them, and re-layouts  1.67 us

profile of v1, /device:TPU:3, one launch (start us, length us, event | category | flops | bytes accessed | tf_op | source)
XLA Modules:
  0.0 71.9 jit_solution(4476972486049126357)
XLA Ops:
  0.7 69.5 %candidate_layer.1 = bf16[128,1024]{1,0:T(8,128)(2,1)} custom-call(s32[1]{0:T(128)S(6)} %copy.10.length_ref, bf16[128,1024]{1,0:T(8,128)(2,1)} %cand_ref.1, s32[1,128]{1,0:T(1,128)} %bitcast.1, bf16[1024,1024]{1,0:T(8,128)(2,1)} %wq_hbm.1, bf16[1024,1024]{1,0:T(8,128)(2,1)} %wg_hbm.1, bf16[1024,1024]{1,0:T(8,128)(2,1)} %wo_hbm.1, ...), custom_call_target="tpu_custom_call" | custom-call | tf_op jit(solution)/shard_map/candidate_layer/pallas_call | solution.py:314
  70.2 1.7 %copy.11 = bf16[128,1024]{1,0:T(8,128)(2,1)} copy(bf16[128,1024]{1,0:T(8,128)(2,1)} %candidate_layer.1) | data formatting | bytes 524288

commit v2 on v0

v2 whole, which is shorter than its diff:
```python
import functools

import jax
import jax.numpy as jnp
from jax import lax
from jax.experimental import pallas as pl
from jax.experimental.pallas import tpu as pltpu
from jax.sharding import PartitionSpec as P

HEADS = 8
CAP = 8
FOLD = 2
PIECE = CAP * FOLD
RING = 4
GROUPS = HEADS // FOLD
RAW = 2
OWN, NEAR, FAR, REST = range(RING)
EVENT_BLOCK = 1024
MESH = pl.DeviceIdType.MESH
F32 = jnp.float32
BF16 = jnp.bfloat16


def dot(a, b):
    return jnp.dot(a, b, preferred_element_type=F32)


def layer_kernel(
    owners,
    length_ref, cand_ref, route_ref, wq_hbm, wg_hbm, wo_hbm, k_hbm, v_hbm,
    out_ref,
    keys, raw, vt, wq, wg, wo, fold, wide, rawq, seats, xc, part, pf, late, sums, gl, gr, rl, rr, tot, ret,
    gate,
    load_sem, in_send, in_recv, w_send, w_recv, x_send, x_recv, p_send, p_recv, r_send, r_recv,
):
    me = lax.axis_index("owner")
    seq = lax.axis_index("seq")
    right, left = lax.rem(seq + 1, RING), lax.rem(seq + RING - 1, RING)
    per = owners // 4
    rows, width = cand_ref.shape
    head = width // HEADS
    events = keys.shape[0]
    block = min(EVENT_BLOCK, events)
    blocks = events // block
    span = per * CAP

    half = width // FOLD
    lead = [(slice(None), slice(f * half, f * half + head)) for f in range(FOLD)]
    rest = [(slice(None), slice(f * half + head, (f + 1) * half)) for f in range(FOLD)]
    loads = [
        pltpu.make_async_copy(src, dst, load_sem.at[i])
        for i, (src, dst) in enumerate(
            [(wq_hbm.at[part_of], wq.at[part_of]) for part_of in lead + rest]
            + [(v_hbm.at[0], raw), (wg_hbm, wg), (k_hbm.at[0], keys), (wo_hbm, wo)]
        )
    ]
    load_wq, (load_v, load_wg, load_k, load_wo) = loads[:2 * FOLD], loads[2 * FOLD:]
    for load in loads:
        load.start()

    barrier = pltpu.get_barrier_semaphore()

    def greet(i, carry):
        other = lax.rem(me + i, owners)
        pl.semaphore_signal(barrier, inc=1, device_id=(other, seq), device_id_type=MESH)
        return carry

    lax.fori_loop(1, owners, greet, 0)
    for other in (left, right):
        pl.semaphore_signal(barrier, inc=1, device_id=(me, other), device_id_type=MESH)

    def remote(src, dst, send, recv, owner, place):
        return pltpu.make_async_remote_copy(
            src_ref=src, dst_ref=dst, send_sem=send, recv_sem=recv,
            device_id=(owner, place), device_id_type=MESH,
        )

    def await_bytes(ref, sem):
        pltpu.make_async_copy(ref, ref, sem).wait()

    route_lane = jnp.broadcast_to(route_ref[...].astype(F32), (rows, rows))
    route_row = jnp.transpose(route_lane)
    lane = lax.broadcasted_iota(jnp.int32, (rows, rows), 1)
    sub = lax.broadcasted_iota(jnp.int32, (rows, rows), 0)
    same = route_lane == route_row
    before = jnp.sum(jnp.where(same & (sub < lane), 1.0, 0.0), axis=0, keepdims=True)
    place_lane = (route_ref[...].astype(F32) * PIECE + before).astype(jnp.int32)
    slot = lax.broadcasted_iota(jnp.int32, (owners * PIECE, rows), 0)

    scale = 0.5 * head ** (-0.5)

    def project(f, low, high):
        at = slice(f * half + low * head, f * half + high * head)
        return (dot(cand_ref[...], wq[:, at]) * scale).astype(BF16)

    def pack(places, queries):
        return sum(
            dot(jnp.where(slot == places + CAP * f, 1.0, 0.0).astype(BF16), queries[f])
            for f in range(FOLD)
        ).astype(BF16)

    for load in load_wq[:FOLD]:
        load.wait()
    fold[0] = pack(place_lane, [project(f, 0, 1) for f in range(FOLD)])

    pl.semaphore_wait(barrier, owners + 1)

    def piece(ref, g, owner):
        return ref.at[g, pl.ds(pl.multiple_of(owner * PIECE, PIECE), PIECE), :]

    def scatter(g):
        home = xc.at[g, me, seq]

        def send(i, carry):
            other = lax.rem(me + i, owners)
            remote(piece(fold, g, other), home, in_send.at[g], in_recv.at[g], other, seq).start()
            return carry

        lax.fori_loop(1, owners, send, 0)
        pltpu.make_async_copy(piece(fold, g, me), home, in_recv.at[g]).start()

    def await_own(g):
        await_bytes(xc.at[g, :, 0], in_recv.at[g])

    def pass_raw(kind, ref, place):
        remote(ref, ref, w_send.at[kind], w_recv.at[kind], me, place).start()

    def raw_near():
        pass_raw(0, rawq.at[seq], right)
        pass_raw(1, rawq.at[seq], left)
        pass_raw(2, seats.at[seq], right)
        pass_raw(3, seats.at[seq], left)

    lower, upper = pl.ds(0, rows // 2), pl.ds(rows // 2, rows // 2)

    def raw_far():
        for kind in range(2):
            await_bytes(rawq.at[0], w_recv.at[kind])
        for kind in range(2, 4):
            await_bytes(seats.at[0], w_recv.at[kind])
        pass_raw(4, rawq.at[left, lower], right)
        pass_raw(5, rawq.at[right, upper], left)
        pass_raw(6, seats.at[left], right)

    def scatter_raw():
        for kind in range(4, 6):
            await_bytes(rawq.at[0, lower], w_recv.at[kind])
        await_bytes(seats.at[0], w_recv.at[6])
        for s in range(RING):
            queries = [rawq[s, :, f * head:(f + 1) * head] for f in range(FOLD)]
            packed = pack(seats[s, 0:1, :].astype(jnp.int32), queries)
            wide[:, s] = packed.reshape(owners, PIECE, head)

        def send(i, carry):
            other = lax.rem(me + i, owners)
            remote(
                wide.at[other], xc.at[RAW, me], in_send.at[RAW], in_recv.at[RAW], other, seq
            ).start()
            return carry

        lax.fori_loop(1, owners, send, 0)
        pltpu.make_async_copy(wide.at[me], xc.at[RAW, me], in_recv.at[RAW]).start()

    def await_raw():
        await_bytes(xc.at[RAW], in_recv.at[RAW])

    first, last = pl.ds(0, 2), pl.ds(2, 2)
    low, high = pl.ds(0, owners // 2), pl.ds(owners // 2, owners // 2)

    def pass_on(g, kind, which, source, place):
        ref = xc.at[g, which, source]
        remote(
            ref, ref, x_send.at[g * 6 + kind], x_recv.at[g * 6 + kind], me, place
        ).start()

    def pass_near(g):
        pass_on(g, 0, low, seq, right)
        pass_on(g, 1, high, seq, left)

    def pass_rest(g):
        pass_on(g, 4, high, seq, right)
        pass_on(g, 5, low, seq, left)

    def pass_far(g):
        pass_on(g, 2, low, left, right)
        pass_on(g, 3, high, right, left)

    def await_pair(g, kind):
        await_bytes(xc.at[g, low, 0], x_recv.at[g * 6 + kind])

    def await_near(g):
        await_pair(g, 0)
        await_pair(g, 1)

    def await_far(g):
        await_pair(g, 2)
        await_pair(g, 3)

    def await_rest(g):
        await_pair(g, 4)
        await_pair(g, 5)

    def give(g, kind, source, pair, dest, place):
        remote(
            part.at[g, source, pair], dest, p_send.at[g * 6 + kind], p_recv.at[g * 6 + kind],
            me, place,
        ).start()

    def give_near(g):
        give(g, 0, NEAR, last, gl.at[g, last], right)
        give(g, 1, NEAR, first, gr.at[g, first], left)

    def give_far(g):
        give(g, 2, FAR, first, rl.at[g], right)
        give(g, 3, FAR, last, rr.at[g], left)

    def await_part(g, kind):
        await_bytes(rl.at[g], p_recv.at[g * 6 + kind])

    def give_rest(g):
        await_part(g, 2)
        part[g, REST, 0:2] = (part[g, REST, 0:2].astype(F32) + rl[g].astype(F32)).astype(BF16)
        give(g, 4, REST, first, gl.at[g, first], right)
        await_part(g, 3)
        part[g, REST, 2:4] = (part[g, REST, 2:4].astype(F32) + rr[g].astype(F32)).astype(BF16)
        give(g, 5, REST, last, gr.at[g, last], left)

    def hand_back(pair):
        for g in (2 * pair, 2 * pair + 1):
            for kind in (0, 1, 4, 5):
                await_part(g, kind)
            total = part[g, OWN].astype(F32) + gl[g].astype(F32) + gr[g].astype(F32)
            at = slice(g % 2 * head, (g % 2 + 1) * head)
            tot[pair, :, at] = total.astype(BF16).reshape(owners * PIECE, head)
        landing = piece(ret, pair, me)

        def send(i, carry):
            other = lax.rem(me + i, owners)
            remote(
                piece(tot, pair, other), landing, r_send.at[pair], r_recv.at[pair], other, seq
            ).start()
            return carry

        lax.fori_loop(1, owners, send, 0)
        pltpu.make_async_copy(piece(tot, pair, me), landing, r_recv.at[pair]).start()

    def turn(g):
        limit = length_ref[0] - seq * events

        def some(i, carry):
            at = pl.ds(pl.multiple_of(i * block, block), block)
            event = i * block + lax.broadcasted_iota(jnp.int32, (block, head), 0)
            for f in range(FOLD):
                cols = slice((f * GROUPS + g) * head, (f * GROUPS + g + 1) * head)
                values = jnp.where(event < limit, raw[at, cols].astype(F32), 0.0)
                vt[cols, at] = jnp.transpose(values).astype(BF16)
            return carry

        lax.fori_loop(0, blocks, some, 0)

    def unit(n):
        early = 1 - n // 8
        step, turned = lax.rem(n, 4), lax.div(jnp.maximum(n, 8) - 8, 2)
        early_chunk = step + step // 2 * (1 - 2 * lax.rem(step, 2))
        late_chunk = 2 + turned - 3 * (turned // 2) - 2 * (turned // 3)
        return (
            early * (n // 4) + (1 - early) * (2 + lax.rem(n, 2)),
            early * early_chunk + (1 - early) * late_chunk,
        )

    def cols(g, f):
        return pl.ds(pl.multiple_of((f * GROUPS + g) * head, head), head)

    def finish(f, total):
        back = jnp.transpose(total)
        for j in range(4):
            pf[j, :, f] = back[j * span:(j + 1) * span].reshape(per, CAP, head)

    def settle(g, f, e, weight):
        return dot(vt[cols(g, f), e * block:(e + 1) * block], weight)

    def settle_late(g, c):
        finish(FOLD - 1, sums[...] + settle(g, FOLD - 1, blocks - 1, late[...]))
        part[g, c] = pf[...].reshape(4, per * PIECE, head).astype(BF16)

    def attend(n):
        g, c = unit(n)

        before, after = lax.rem(seq - c + RING, RING), lax.rem(seq + c, RING)

        def columns(f):
            parts = [
                xc[g, which, s].astype(F32).reshape(-1, FOLD, CAP, head)[:, f].reshape(-1, head)
                for which, s in ((low, before), (high, after))
            ]
            return jnp.transpose(jnp.concatenate(parts, axis=0)).astype(BF16)

        def weigh(f, e, turned):
            score = dot(keys[e * block:(e + 1) * block, cols(g, f)], turned)
            return (score + score * jnp.tanh(score)).astype(BF16)

        turned = [columns(f) for f in range(FOLD)]
        waiting = None
        total = None
        for f in range(FOLD):
            for e in range(blocks):
                weight = weigh(f, e, turned[f])
                if waiting is None:
                    settle_late(*unit(jnp.maximum(n - 1, 0)))
                else:
                    term = settle(g, *waiting)
                    total = term if waiting[1] == 0 else total + term
                    if waiting[1] == blocks - 1:
                        finish(waiting[0], total)
                waiting = (f, e, weight)
        sums[...] = total
        late[...] = waiting[2]

    def run(count, after):
        def step(n, carry):
            attend(n)
            def pick(acts, start, stop):
                if stop - start == 1:
                    for act, *args in acts[start]:
                        act(*args)
                    return
                mid = (start + stop) // 2
                for test, lo, hi in ((n < mid, start, mid), (n >= mid, mid, stop)):
                    some = {k: v for k, v in acts.items() if lo <= k < hi}
                    if some:
                        pl.when(test)(functools.partial(pick, some, lo, hi))

            pick(after, 0, count)
            return carry

        lax.fori_loop(0, count, step, 0)

    def gates():
        load_wg.wait()
        gated = dot(cand_ref[...], wg[...])
        gate[...] = gated / (1.0 + jnp.exp(-gated))

    scatter(0)
    for load in load_wq[FOLD:]:
        load.wait()
    others = [project(f, 1, GROUPS) for f in range(FOLD)]
    for f in range(FOLD):
        rawq[seq, :, f * head:(f + 1) * head] = others[f][:, (RAW - 1) * head:RAW * head]
    seats[seq] = jnp.broadcast_to(place_lane.astype(F32), (8, rows))
    raw_near()
    packed = pack(place_lane, others)
    for g in range(1, GROUPS):
        if g != RAW:
            fold[g] = packed[:, (g - 1) * head:g * head]
            scatter(g)
    late[...] = jnp.zeros_like(late)
    sums[...] = jnp.zeros_like(sums)
    load_v.wait()
    turn(0)
    turn(1)
    gates()
    await_own(0)
    pass_near(0)
    pass_rest(0)
    load_k.wait()
    run(4 * GROUPS, {
        0: [
            (await_own, 1), (pass_near, 1), (raw_far,), (turn, 2), (await_near, 0),
            (pass_far, 0), (pass_rest, 1),
        ],
        1: [(await_rest, 0), (await_own, 3), (pass_near, 3), (turn, 3)],
        2: [
            (give_near, 0), (await_near, 1), (pass_far, 1), (scatter_raw,), (await_far, 0),
            (pass_rest, 3),
        ],
        4: [(give_far, 0), (await_near, 3), (pass_far, 3)],
        5: [(await_rest, 1)],
        6: [(give_near, 1), (await_far, 1)],
        7: [(give_rest, 0), (await_raw,)],
        8: [(give_far, 1), (await_far, 3)],
        9: [(give_far, 2)],
        10: [(give_far, 3), (await_rest, 3)],
        11: [(give_rest, 1)],
        12: [(give_rest, 2)],
        13: [(give_near, 2), (give_rest, 3)],
        14: [(give_near, 3), (hand_back, 0)],
    })
    settle_late(*unit(4 * GROUPS - 1))
    hand_back(1)

    place_row = jnp.transpose(
        jnp.broadcast_to(place_lane.astype(F32), (rows, rows))
    ).astype(jnp.int32)[:, :1]
    slot_lane = lax.broadcasted_iota(jnp.int32, (rows, owners * PIECE), 1)
    picks = [
        jnp.where(slot_lane == place_row + CAP * f, 1.0, 0.0).astype(BF16) for f in range(FOLD)
    ]
    load_wo.wait()

    for pair in range(GROUPS // 2):
        await_bytes(ret.at[pair], r_recv.at[pair])
    attended = jnp.concatenate(
        [dot(pick, ret[pair]) for pick in picks for pair in range(GROUPS // 2)], axis=1
    )
    centred = attended - jnp.mean(attended, axis=1, keepdims=True)
    normed = centred * lax.rsqrt(jnp.mean(centred * centred, axis=1, keepdims=True) + 1e-05)
    mixed = (normed * gate[...]).astype(BF16)
    out_ref[...] = dot(mixed, wo[...])

    sent = pl.ds(0, (owners - 1) * PIECE)
    for pair in range(GROUPS // 2):
        await_bytes(tot.at[pair, sent], r_send.at[pair])
    await_bytes(wide.at[pl.ds(0, owners - 1)], in_send.at[RAW])
    for kind in range(2):
        await_bytes(rawq.at[0], w_send.at[kind])
    for kind in range(4, 6):
        await_bytes(rawq.at[0, lower], w_send.at[kind])
    for kind in (2, 3, 6):
        await_bytes(seats.at[0], w_send.at[kind])
    for g in range(GROUPS):
        for kind in range(6):
            await_bytes(part.at[g, OWN, first], p_send.at[g * 6 + kind])
            if g != RAW:
                await_bytes(xc.at[g, low, 0], x_send.at[g * 6 + kind])
        if g != RAW:
            await_bytes(fold.at[g, sent], in_send.at[g])


def body(cand, route, lengths, keys, values, wq, wg, wo):
    owners = lax.axis_size("owner")
    rows, width = cand.shape
    head = width // HEADS
    events = keys.shape[1]
    per = owners // 4
    square = pltpu.VMEM((width, width), BF16)
    slots = pltpu.VMEM((GROUPS, owners * PIECE, head), BF16)
    pairs = pltpu.VMEM((GROUPS // 2, owners * PIECE, 2 * head), BF16)
    blocks = lambda *lead: pltpu.VMEM((GROUPS, *lead, per * PIECE, head), BF16)
    sems = lambda n: pltpu.SemaphoreType.DMA((n,))
    vmem = pl.BlockSpec(memory_space=pltpu.VMEM)
    hbm = pl.BlockSpec(memory_space=pl.ANY)
    change = pl.pallas_call(
        functools.partial(layer_kernel, owners),
        out_shape=jax.ShapeDtypeStruct((rows, width), F32),
        in_specs=[pl.BlockSpec(memory_space=pltpu.SMEM), vmem, vmem, hbm, hbm, hbm, hbm, hbm],
        out_specs=vmem,
        scratch_shapes=[
            pltpu.VMEM((events, width), BF16),
            pltpu.VMEM((events, width), BF16),
            pltpu.VMEM((width, events), BF16),
            square, square, square,
            slots,
            pltpu.VMEM((owners, RING, PIECE, head), BF16),
            pltpu.VMEM((RING, rows, FOLD * head), BF16),
            pltpu.VMEM((RING, 8, rows), F32),
            pltpu.VMEM((GROUPS, owners, RING, PIECE, head), BF16),
            blocks(4, 4),
            pltpu.VMEM((4, per, FOLD, CAP, head), F32),
            pltpu.VMEM((min(EVENT_BLOCK, events), 4 * per * CAP), BF16),
            pltpu.VMEM((head, 4 * per * CAP), F32),
            blocks(4), blocks(4), blocks(2), blocks(2),
            pairs,
            pairs,
            pltpu.VMEM((rows, width), F32),
            sems(8), sems(GROUPS), sems(GROUPS), sems(7), sems(7), sems(6 * GROUPS), sems(6 * GROUPS),
            sems(6 * GROUPS), sems(6 * GROUPS), sems(2), sems(2),
        ],
        compiler_params=pltpu.CompilerParams(
            collective_id=0, has_side_effects=True, vmem_limit_bytes=56 * 2**20
        ),
        name="candidate_layer",
    )(lengths, cand, route.reshape(1, rows), wq, wg, wo, keys, values)
    return (cand.astype(F32) + change).astype(BF16)


def solution(mesh):
    placed = (
        P(("owner", "seq"), None),
        P(("owner", "seq")),
        P("owner"),
        P("owner", "seq", None),
        P("owner", "seq", None),
        P(),
        P(),
        P(),
    )
    return jax.shard_map(
        body, mesh=mesh, in_specs=placed, out_specs=P(("owner", "seq"), None), check_vma=False
    )
```

time: 262 us -> 65 us (0.25)
  matrix products: 89.5 us -> 0 us
  Pallas kernels: 0 us -> 62.4 us
  local copies, waits for them, and re-layouts: 61.6 us -> 0.01 us
  waiting for transfers between devices: 52.3 us -> 0 us
  blocking collectives: 20.9 us -> 0 us
  other arithmetic: 15.5 us -> 1.8 us
  between operations: 13.5 us -> 0.68 us
  starting transfers between devices: 7.66 us -> 0 us
    dot_general x10 -> x0, matrix products: 89.5 us -> none  [the longest x8 83.4 us: add_block(): jnp.einsum('hce,ehd->chd', weight, value_part, preferred_element_type=jnp...]
    pallas_call x0 -> x1, Pallas kernels: none -> 62.4 us  [body(): pl.pallas_call(functools.partial(layer_kernel, owners), out_shape=jax.Sha...]
    dynamic_slice x16 -> x0, local copies, waits for them, and re-layouts: 33.2 us -> none  [the longest x8 21.4 us: add_block(): key_part = key_blocks[block_id]]
    reduce_scatter x1 -> x0, waiting for transfers between devices: 29.9 us -> none  [body(): lax.psum_scatter(terms.astype(jnp.bfloat16), 'seq', scatter_dimension=0,...]
    unnamed x15 -> x2, local copies, waits for them, and re-layouts: 21.7 us -> 0.01 us
    all_to_all x1 -> x0, blocking collectives: 20.9 us -> none  [body(): lax.all_to_all(outgoing, 'owner', split_axis=0, concat_axis=0, tiled=True)]
    all_to_all x1 -> x0, waiting for transfers between devices: 11.6 us -> none  [body(): lax.all_to_all(finished, 'owner', split_axis=0, concat_axis=0, tiled=True)]
    all_gather x1 -> x0, waiting for transfers between devices: 10.8 us -> none  [body(): lax.all_gather(query, 'seq', axis=0, tiled=True)]
  transfers between devices with their start and end apart: 3 -> 0, of which waited for: 3 -> 0; matrix products, arithmetic and copies ran while one was open for 7% -> 0% of each run, Pallas kernels for 0% -> 0%
where the time goes in v2:
time: 65 us; the launch traced here: 64.9 us
  Pallas kernels  62.4 us (96%)
  other arithmetic  1.8 us (3%)
  between operations  0.68 us (1%)
    pallas_call x1, Pallas kernels, body(): pl.pallas_call(functools.partial(layer_kernel, owners), out_shape=jax.Sha...  62.4 us
    convert_element_type x1, other arithmetic, body(): return (cand.astype(F32) + change).astype(BF16)  1.8 us

profile of v2, /device:TPU:1, one launch (start us, length us, event | category | flops | bytes accessed | tf_op | source)
XLA Modules:
  0.0 64.9 jit_solution(160356600271615035)
XLA Ops:
  0.7 0.0 copy-start
  0.7 62.4 %candidate_layer.1 = f32[128,1024]{1,0:T(8,128)} custom-call(s32[1]{0:T(128)S(6)} %copy.9.length_ref, bf16[128,1024]{1,0:T(8,128)(2,1)} %cand_ref.1, s32[1,128]{1,0:T(1,128)} %bitcast.1, bf16[1024,1024]{1,0:T(8,128)(2,1)} %wq_hbm.1, bf16[1024,1024]{1,0:T(8,128)(2,1)} %wg_hbm.1, bf16[1024,1024]{1,0:T(8,128)(2,1)} %wo_hbm.1, bf16[1,4096,1024]{2,1,0:T(8,128)(2,1)} %k_hbm.1, ...), custom_call_target="tpu_custom_call" | custom-call | tf_op jit(solution)/shard_map/candidate_layer/pallas_call | solution.py:442
  63.1 0.0 copy-done
  63.1 1.8 %add_convert_fusion = bf16[128,1024]{1,0:T(8,128)(2,1)} fusion(f32[128,1024]{1,0:T(8,128)} %candidate_layer.1, bf16[128,1024]{1,0:T(8,128)(2,1)S(1)} %copy-done), kind=kLoop, calls=%fused_computation | loop fusion | flops 393216 | bytes 1048576 | tf_op jit(solution)/shard_map/convert_element_type | solution.py:473
Async XLA Ops:
  0.7 62.4 %copy-start = (bf16[128,1024]{1,0:T(8,128)(2,1)S(1)}, bf16[128,1024]{1,0:T(8,128)(2,1)}, u32[]{:S(2)}) copy-start(bf16[128,1024]{1,0:T(8,128)(2,1)} %cand_ref.1) | copy-start | bytes 786436

commit v3 on v2

--- a/solution.py
+++ b/solution.py
@@ -258,16 +258,6 @@
 
         lax.fori_loop(0, blocks, some, 0)
 
-    def unit(n):
-        early = 1 - n // 8
-        step, turned = lax.rem(n, 4), lax.div(jnp.maximum(n, 8) - 8, 2)
-        early_chunk = step + step // 2 * (1 - 2 * lax.rem(step, 2))
-        late_chunk = 2 + turned - 3 * (turned // 2) - 2 * (turned // 3)
-        return (
-            early * (n // 4) + (1 - early) * (2 + lax.rem(n, 2)),
-            early * early_chunk + (1 - early) * late_chunk,
-        )
-
     def cols(g, f):
         return pl.ds(pl.multiple_of((f * GROUPS + g) * head, head), head)
 
@@ -283,9 +273,7 @@
         finish(FOLD - 1, sums[...] + settle(g, FOLD - 1, blocks - 1, late[...]))
         part[g, c] = pf[...].reshape(4, per * PIECE, head).astype(BF16)
 
-    def attend(n):
-        g, c = unit(n)
-
+    def attend(g, c, last_g, last_c):
         before, after = lax.rem(seq - c + RING, RING), lax.rem(seq + c, RING)
 
         def columns(f):
@@ -293,20 +281,23 @@
                 xc[g, which, s].astype(F32).reshape(-1, FOLD, CAP, head)[:, f].reshape(-1, head)
                 for which, s in ((low, before), (high, after))
             ]
-            return jnp.transpose(jnp.concatenate(parts, axis=0)).astype(BF16)
-
-        def weigh(f, e, turned):
-            score = dot(keys[e * block:(e + 1) * block, cols(g, f)], turned)
+            return jnp.concatenate(parts, axis=0).astype(BF16)
+
+        def weigh(f, e, queries):
+            score = lax.dot_general(
+                keys[e * block:(e + 1) * block, cols(g, f)], queries, (((1,), (1,)), ((), ())),
+                preferred_element_type=F32,
+            )
             return (score + score * jnp.tanh(score)).astype(BF16)
 
-        turned = [columns(f) for f in range(FOLD)]
+        queries = [columns(f) for f in range(FOLD)]
         waiting = None
         total = None
         for f in range(FOLD):
             for e in range(blocks):
-                weight = weigh(f, e, turned[f])
+                weight = weigh(f, e, queries[f])
                 if waiting is None:
-                    settle_late(*unit(jnp.maximum(n - 1, 0)))
+                    settle_late(last_g, last_c)
                 else:
                     term = settle(g, *waiting)
                     total = term if waiting[1] == 0 else total + term
@@ -316,9 +307,17 @@
         sums[...] = total
         late[...] = waiting[2]
 
-    def run(count, after):
+    def run(units, lates, after):
+        def digits(values):
+            numbers = [values[i:i + 8] for i in range(0, len(values), 8)]
+            return [sum(v * 4 ** i for i, v in enumerate(number)) for number in numbers]
+
+        columns = list(zip(*units)) + list(zip(*lates))
+        numbers = [digits(column) for column in columns]
+
         def step(n, carry):
-            attend(n)
+            attend(*[lax.rem(number, 4) for number in carry])
+
             def pick(acts, start, stop):
                 if stop - start == 1:
                     for act, *args in acts[start]:
@@ -330,10 +329,14 @@
                     if some:
                         pl.when(test)(functools.partial(pick, some, lo, hi))
 
-            pick(after, 0, count)
-            return carry
-
-        lax.fori_loop(0, count, step, 0)
+            pick(after, 0, len(units))
+            turn_over = (n + 1) // 8 - n // 8
+            return tuple(
+                number // 4 + turn_over * second
+                for number, (_, second) in zip(carry, numbers)
+            )
+
+        lax.fori_loop(0, len(units), step, tuple(jnp.int32(first) for first, _ in numbers))
 
     def gates():
         load_wg.wait()
@@ -356,36 +359,39 @@
     late[...] = jnp.zeros_like(late)
     sums[...] = jnp.zeros_like(sums)
     load_v.wait()
-    turn(0)
-    turn(1)
+    for g in range(GROUPS):
+        turn(g)
     gates()
     await_own(0)
     pass_near(0)
     pass_rest(0)
     load_k.wait()
-    run(4 * GROUPS, {
-        0: [
-            (await_own, 1), (pass_near, 1), (raw_far,), (turn, 2), (await_near, 0),
-            (pass_far, 0), (pass_rest, 1),
+    units = [
+        (0, OWN), (1, OWN), (0, NEAR), (0, REST), (1, NEAR), (0, FAR), (1, REST), (1, FAR),
+        (3, FAR), (3, REST), (2, FAR), (2, REST), (3, NEAR), (2, NEAR), (3, OWN), (2, OWN),
+    ]
+    lates = [units[0]] + units[:-1]
+    lates[14] = units[15]
+    run(units, lates, {
+        0: [(await_own, 1), (pass_near, 1), (raw_far,)],
+        1: [
+            (await_near, 0), (pass_far, 0), (pass_rest, 1), (await_own, 3),
+            (pass_near, 3),
         ],
-        1: [(await_rest, 0), (await_own, 3), (pass_near, 3), (turn, 3)],
-        2: [
-            (give_near, 0), (await_near, 1), (pass_far, 1), (scatter_raw,), (await_far, 0),
-            (pass_rest, 3),
-        ],
-        4: [(give_far, 0), (await_near, 3), (pass_far, 3)],
-        5: [(await_rest, 1)],
-        6: [(give_near, 1), (await_far, 1)],
-        7: [(give_rest, 0), (await_raw,)],
-        8: [(give_far, 1), (await_far, 3)],
-        9: [(give_far, 2)],
-        10: [(give_far, 3), (await_rest, 3)],
-        11: [(give_rest, 1)],
-        12: [(give_rest, 2)],
-        13: [(give_near, 2), (give_rest, 3)],
-        14: [(give_near, 3), (hand_back, 0)],
+        2: [(await_rest, 0)],
+        3: [(give_near, 0), (await_near, 1), (pass_far, 1), (scatter_raw,)],
+        4: [(await_far, 0), (await_near, 3), (pass_far, 3), (pass_rest, 3)],
+        5: [(await_rest, 1), (give_near, 1)],
+        6: [(give_far, 0), (await_far, 1)],
+        7: [(await_far, 3)],
+        8: [(give_far, 1), (await_rest, 3)],
+        9: [(give_far, 3), (give_rest, 0), (await_raw,)],
+        11: [(give_far, 2), (give_rest, 1)],
+        12: [(give_rest, 3)],
+        13: [(settle_late, *units[13]), (give_near, 3), (give_near, 2)],
+        14: [(give_rest, 2), (hand_back, 0)],
     })
-    settle_late(*unit(4 * GROUPS - 1))
+    settle_late(*units[15])
     hand_back(1)
 
     place_row = jnp.transpose(

time: 65 us -> 62.5 us (0.962)
  Pallas kernels: 62.4 us -> 59.9 us
    pallas_call x1, Pallas kernels: 62.4 us -> 59.9 us  [body(): pl.pallas_call(functools.partial(layer_kernel, owners), out_shape=jax.Sha...]
where the time goes in v3:
time: 62.5 us; the launch traced here: 62.4 us
  Pallas kernels  59.9 us (96%)
  other arithmetic  1.8 us (3%)
  between operations  0.68 us (1%)
    pallas_call x1, Pallas kernels, body(): pl.pallas_call(functools.partial(layer_kernel, owners), out_shape=jax.Sha...  59.9 us
    convert_element_type x1, other arithmetic, body(): return (cand.astype(F32) + change).astype(BF16)  1.8 us

profile of v3, /device:TPU:1, one launch (start us, length us, event | category | flops | bytes accessed | tf_op | source)
XLA Modules:
  0.0 62.4 jit_solution(3487484064363418729)
XLA Ops:
  0.7 0.0 copy-start
  0.7 59.9 %candidate_layer.1 = f32[128,1024]{1,0:T(8,128)} custom-call(s32[1]{0:T(128)S(6)} %copy.9.length_ref, bf16[128,1024]{1,0:T(8,128)(2,1)} %cand_ref.1, s32[1,128]{1,0:T(1,128)} %bitcast.1, bf16[1024,1024]{1,0:T(8,128)(2,1)} %wq_hbm.1, bf16[1024,1024]{1,0:T(8,128)(2,1)} %wg_hbm.1, bf16[1024,1024]{1,0:T(8,128)(2,1)} %wo_hbm.1, bf16[1,4096,1024]{2,1,0:T(8,128)(2,1)} %k_hbm.1, ...), custom_call_target="tpu_custom_call" | custom-call | tf_op jit(solution)/shard_map/candidate_layer/pallas_call | solution.py:448
  60.5 0.0 copy-done
  60.6 1.8 %add_convert_fusion = bf16[128,1024]{1,0:T(8,128)(2,1)} fusion(f32[128,1024]{1,0:T(8,128)} %candidate_layer.1, bf16[128,1024]{1,0:T(8,128)(2,1)S(1)} %copy-done), kind=kLoop, calls=%fused_computation | loop fusion | flops 393216 | bytes 1048576 | tf_op jit(solution)/shard_map/convert_element_type | solution.py:479
Async XLA Ops:
  0.7 59.9 %copy-start = (bf16[128,1024]{1,0:T(8,128)(2,1)S(1)}, bf16[128,1024]{1,0:T(8,128)(2,1)}, u32[]{:S(2)}) copy-start(bf16[128,1024]{1,0:T(8,128)(2,1)} %cand_ref.1) | copy-start | bytes 786436

commit v4 on v3

--- a/solution.py
+++ b/solution.py
@@ -249,11 +249,11 @@
 
         def some(i, carry):
             at = pl.ds(pl.multiple_of(i * block, block), block)
-            event = i * block + lax.broadcasted_iota(jnp.int32, (block, head), 0)
+            event = i * block + lax.broadcasted_iota(jnp.int32, (1, block), 1)
+            kept = jnp.where(event < limit, 1.0, 0.0).astype(BF16)
             for f in range(FOLD):
                 cols = slice((f * GROUPS + g) * head, (f * GROUPS + g + 1) * head)
-                values = jnp.where(event < limit, raw[at, cols].astype(F32), 0.0)
-                vt[cols, at] = jnp.transpose(values).astype(BF16)
+                vt[cols, at] = jnp.transpose(raw[at, cols]) * kept
             return carry
 
         lax.fori_loop(0, blocks, some, 0)
@@ -361,7 +361,6 @@
     load_v.wait()
     for g in range(GROUPS):
         turn(g)
-    gates()
     await_own(0)
     pass_near(0)
     pass_rest(0)
@@ -394,28 +393,7 @@
     settle_late(*units[15])
     hand_back(1)
 
-    place_row = jnp.transpose(
-        jnp.broadcast_to(place_lane.astype(F32), (rows, rows))
-    ).astype(jnp.int32)[:, :1]
-    slot_lane = lax.broadcasted_iota(jnp.int32, (rows, owners * PIECE), 1)
-    picks = [
-        jnp.where(slot_lane == place_row + CAP * f, 1.0, 0.0).astype(BF16) for f in range(FOLD)
-    ]
-    load_wo.wait()
-
-    for pair in range(GROUPS // 2):
-        await_bytes(ret.at[pair], r_recv.at[pair])
-    attended = jnp.concatenate(
-        [dot(pick, ret[pair]) for pick in picks for pair in range(GROUPS // 2)], axis=1
-    )
-    centred = attended - jnp.mean(attended, axis=1, keepdims=True)
-    normed = centred * lax.rsqrt(jnp.mean(centred * centred, axis=1, keepdims=True) + 1e-05)
-    mixed = (normed * gate[...]).astype(BF16)
-    out_ref[...] = dot(mixed, wo[...])
-
     sent = pl.ds(0, (owners - 1) * PIECE)
-    for pair in range(GROUPS // 2):
-        await_bytes(tot.at[pair, sent], r_send.at[pair])
     await_bytes(wide.at[pl.ds(0, owners - 1)], in_send.at[RAW])
     for kind in range(2):
         await_bytes(rawq.at[0], w_send.at[kind])
@@ -430,6 +408,27 @@
                 await_bytes(xc.at[g, low, 0], x_send.at[g * 6 + kind])
         if g != RAW:
             await_bytes(fold.at[g, sent], in_send.at[g])
+    gates()
+    place_row = jnp.transpose(
+        jnp.broadcast_to(place_lane.astype(F32), (rows, rows))
+    ).astype(jnp.int32)[:, :1]
+    slot_lane = lax.broadcasted_iota(jnp.int32, (rows, owners * PIECE), 1)
+    picks = [
+        jnp.where(slot_lane == place_row + CAP * f, 1.0, 0.0).astype(BF16) for f in range(FOLD)
+    ]
+    load_wo.wait()
+
+    returned = []
+    for pair in range(GROUPS // 2):
+        await_bytes(ret.at[pair], r_recv.at[pair])
+        returned.append([dot(pick, ret[pair]) for pick in picks])
+    attended = jnp.concatenate([rows_of[f] for f in range(FOLD) for rows_of in returned], axis=1)
+    centred = attended - jnp.mean(attended, axis=1, keepdims=True)
+    normed = centred * lax.rsqrt(jnp.mean(centred * centred, axis=1, keepdims=True) + 1e-05)
+    mixed = (normed * gate[...]).astype(BF16)
+    out_ref[...] = (cand_ref[...].astype(F32) + dot(mixed, wo[...])).astype(BF16)
+    for pair in range(GROUPS // 2):
+        await_bytes(tot.at[pair, sent], r_send.at[pair])
 
 
 def body(cand, route, lengths, keys, values, wq, wg, wo):
@@ -445,9 +444,9 @@
     sems = lambda n: pltpu.SemaphoreType.DMA((n,))
     vmem = pl.BlockSpec(memory_space=pltpu.VMEM)
     hbm = pl.BlockSpec(memory_space=pl.ANY)
-    change = pl.pallas_call(
+    return pl.pallas_call(
         functools.partial(layer_kernel, owners),
-        out_shape=jax.ShapeDtypeStruct((rows, width), F32),
+        out_shape=jax.ShapeDtypeStruct((rows, width), BF16),
         in_specs=[pl.BlockSpec(memory_space=pltpu.SMEM), vmem, vmem, hbm, hbm, hbm, hbm, hbm],
         out_specs=vmem,
         scratch_shapes=[
@@ -476,7 +475,6 @@
         ),
         name="candidate_layer",
     )(lengths, cand, route.reshape(1, rows), wq, wg, wo, keys, values)
-    return (cand.astype(F32) + change).astype(BF16)
 
 
 def solution(mesh):

time: 62.5 us -> 62 us (level)
  other arithmetic: 1.8 us -> 0 us
  local copies, waits for them, and re-layouts: 0.01 us -> 1.67 us
    convert_element_type x1 -> x0, other arithmetic: 1.8 us -> none  [body(): return (cand.astype(F32) + change).astype(BF16)]
    unnamed x2 -> x1, local copies, waits for them, and re-layouts: 0.01 us -> 1.67 us
where the time goes in v4:
time: 62 us; the launch traced here: 61.8 us
  Pallas kernels  59.5 us (96%)
  local copies, waits for them, and re-layouts  1.67 us (3%)
  between operations  0.66 us (1%)
    pallas_call x1, Pallas kernels, body(): pl.pallas_call(functools.partial(layer_kernel, owners), out_shape=jax.Sha...  59.5 us
    unnamed x1, local copies, waits for them, and re-layouts  1.67 us

profile of v4, /device:TPU:1, one launch (start us, length us, event | category | flops | bytes accessed | tf_op | source)
XLA Modules:
  0.0 61.8 jit_solution(14264472761795913923)
XLA Ops:
  0.7 59.5 %candidate_layer.1 = bf16[128,1024]{1,0:T(8,128)(2,1)} custom-call(s32[1]{0:T(128)S(6)} %copy.10.length_ref, bf16[128,1024]{1,0:T(8,128)(2,1)} %cand_ref.1, s32[1,128]{1,0:T(1,128)} %bitcast.1, bf16[1024,1024]{1,0:T(8,128)(2,1)} %wq_hbm.1, bf16[1024,1024]{1,0:T(8,128)(2,1)} %wg_hbm.1, bf16[1024,1024]{1,0:T(8,128)(2,1)} %wo_hbm.1, ...), custom_call_target="tpu_custom_call" | custom-call | tf_op jit(solution)/shard_map/candidate_layer/pallas_call | solution.py:447
  60.2 1.7 %copy.11 = bf16[128,1024]{1,0:T(8,128)(2,1)} copy(bf16[128,1024]{1,0:T(8,128)(2,1)} %candidate_layer.1) | data formatting | bytes 524288

commit v5 on v4

--- a/solution.py
+++ b/solution.py
@@ -367,7 +367,7 @@
     load_k.wait()
     units = [
         (0, OWN), (1, OWN), (0, NEAR), (0, REST), (1, NEAR), (0, FAR), (1, REST), (1, FAR),
-        (3, FAR), (3, REST), (2, FAR), (2, REST), (3, NEAR), (2, NEAR), (3, OWN), (2, OWN),
+        (3, FAR), (2, FAR), (3, NEAR), (2, NEAR), (3, REST), (2, REST), (3, OWN), (2, OWN),
     ]
     lates = [units[0]] + units[:-1]
     lates[14] = units[15]
@@ -383,12 +383,13 @@
         5: [(await_rest, 1), (give_near, 1)],
         6: [(give_far, 0), (await_far, 1)],
         7: [(await_far, 3)],
-        8: [(give_far, 1), (await_rest, 3)],
-        9: [(give_far, 3), (give_rest, 0), (await_raw,)],
-        11: [(give_far, 2), (give_rest, 1)],
-        12: [(give_rest, 3)],
-        13: [(settle_late, *units[13]), (give_near, 3), (give_near, 2)],
-        14: [(give_rest, 2), (hand_back, 0)],
+        8: [(give_far, 1), (await_raw,)],
+        9: [(give_far, 3), (give_rest, 0)],
+        10: [(give_far, 2)],
+        11: [(give_near, 3), (give_rest, 1), (await_rest, 3)],
+        12: [(give_near, 2)],
+        13: [(settle_late, *units[13]), (give_rest, 3), (give_rest, 2)],
+        14: [(hand_back, 0)],
     })
     settle_late(*units[15])
     hand_back(1)

time: 62 us -> 61.6 us (level)
  no operation moved by 1% of the time
where the time goes in v5:
time: 61.6 us; the launch traced here: 61.5 us
  Pallas kernels  59.2 us (96%)
  local copies, waits for them, and re-layouts  1.67 us (3%)
  between operations  0.66 us (1%)
    pallas_call x1, Pallas kernels, body(): pl.pallas_call(functools.partial(layer_kernel, owners), out_shape=jax.Sha...  59.2 us
    unnamed x1, local copies, waits for them, and re-layouts  1.67 us

profile of v5, /device:TPU:1, one launch (start us, length us, event | category | flops | bytes accessed | tf_op | source)
XLA Modules:
  0.0 61.5 jit_solution(5653580478668782956)
XLA Ops:
  0.7 59.2 %candidate_layer.1 = bf16[128,1024]{1,0:T(8,128)(2,1)} custom-call(s32[1]{0:T(128)S(6)} %copy.10.length_ref, bf16[128,1024]{1,0:T(8,128)(2,1)} %cand_ref.1, s32[1,128]{1,0:T(1,128)} %bitcast.1, bf16[1024,1024]{1,0:T(8,128)(2,1)} %wq_hbm.1, bf16[1024,1024]{1,0:T(8,128)(2,1)} %wg_hbm.1, bf16[1024,1024]{1,0:T(8,128)(2,1)} %wo_hbm.1, ...), custom_call_target="tpu_custom_call" | custom-call | tf_op jit(solution)/shard_map/candidate_layer/pallas_call | solution.py:448
  59.8 1.7 %copy.11 = bf16[128,1024]{1,0:T(8,128)(2,1)} copy(bf16[128,1024]{1,0:T(8,128)(2,1)} %candidate_layer.1) | data formatting | bytes 524288
